TPU v7x, 32 devices: a whole 2x2x4 slice. The times are simulated.
32 devices in a mesh: head: 2 (over y), seq: 16 (over z, x, core).
Axes of the slice: x: 2, y: 2, z: 4, core: 2. Of those that a mesh axis runs over, the one named last changes fastest.
Arguments:
- query: bfloat16 [16, 1024, 8192], P('seq', 'head'), may hold values from -40 to 40
- key: bfloat16 [16, 1024, 1024], P('seq', 'head'), may hold values from -4 to 4
- value: bfloat16 [16, 1024, 1024], P('seq', 'head'), may hold values from -6 to 6
- output_gradient: bfloat16 [16, 1024, 8192], P('seq', 'head'), may hold values from -6 to 6
- kv_index: int32 [128, 3], replicated, may hold values from 0 to 127, as said below
- count: int32 [128], replicated, may hold values from 1 to 3, as said below
Outputs:
- attn_out: bfloat16 [16, 1024, 8192], P('seq', 'head')
- grad_query: bfloat16 [16, 1024, 8192], P('seq', 'head')
- key_gradient: bfloat16 [16, 1024, 1024], P('seq', 'head')
- value_gradient: bfloat16 [16, 1024, 1024], P('seq', 'head')
Inputs may be any that keep to these rules, and one draw needn't show every extreme that they name: `kv_index`: the first count[i] entries of row i are distinct blocks: i, i-1, down to i-w+1 for some w from 1 to 2, then at most 1 block below i-w+1 that is the last block of some shard (block number ≡ 7 modulo 8). Later entries are arbitrary block numbers. `count`: the number of live entries of each row of kv_index; the last row has 3, the first 1.
All inputs are finite; a program needn't handle non-finite values.
Results may differ from a plain program's by a relative error of at most 0.035.
Values may be sent and summed in bfloat16 or wider, within the bound.
A program may use at most 256 MiB of HBM per device.

v0:
```python
import math

import jax
import jax.numpy as jnp
from jax import lax
from jax.sharding import PartitionSpec as P

QUERY_HEADS = 64
KEY_VALUE_HEADS = 8
HEAD_SIZE = 128
BLOCK_TOKENS = 128
MAXK = 3


def fetch_summaries(key_rows, values):
    rows = key_rows.shape[1]
    last_keys = key_rows[0, rows - BLOCK_TOKENS :, :]
    last_values = values[0, rows - BLOCK_TOKENS :, :]
    return (
        lax.all_gather(last_keys, "seq", axis=0, tiled=True),
        lax.all_gather(last_values, "seq", axis=0, tiled=True),
    )


def sum_summaries(far_keys, far_values):
    return (
        lax.psum_scatter(
            far_keys.astype(jnp.bfloat16), "seq", scatter_dimension=0, tiled=True
        ).astype(jnp.float32),
        lax.psum_scatter(
            far_values.astype(jnp.bfloat16), "seq", scatter_dimension=0, tiled=True
        ).astype(jnp.float32),
    )


def shards(query, key, value, output_gradient, kv_index, count):
    nseq = lax.axis_size("seq")
    shard = lax.axis_index("seq")
    query_rows, key_rows, values, grads = (
        lax.all_to_all(query, "head", split_axis=2, concat_axis=1, tiled=True),
        lax.all_to_all(key, "head", split_axis=2, concat_axis=1, tiled=True),
        lax.all_to_all(value, "head", split_axis=2, concat_axis=1, tiled=True),
        lax.all_to_all(output_gradient, "head", split_axis=2, concat_axis=1, tiled=True),
    )
    summary = fetch_summaries(key_rows, values)
    rows = query_rows.shape[1]
    width_kv = key_rows.shape[2]
    kv_local = width_kv // HEAD_SIZE
    query_group = QUERY_HEADS // KEY_VALUE_HEADS
    nblock = rows // BLOCK_TOKENS
    npool = nblock + nseq
    scale = 1.0 / math.sqrt(HEAD_SIZE)
    pool_keys = jnp.concatenate([key_rows[0], summary[0]], axis=0).reshape(
        npool, BLOCK_TOKENS, kv_local, HEAD_SIZE
    )
    pool_values = jnp.concatenate([values[0], summary[1]], axis=0).reshape(
        npool, BLOCK_TOKENS, kv_local, HEAD_SIZE
    )
    q_blocks = query_rows[0].reshape(nblock, BLOCK_TOKENS, kv_local, query_group, HEAD_SIZE)
    g_blocks = grads[0].reshape(nblock, BLOCK_TOKENS, kv_local, query_group, HEAD_SIZE)
    place = jnp.arange(MAXK, dtype=jnp.int32)
    tokens = jnp.arange(BLOCK_TOKENS, dtype=jnp.int32)
    pool_ids = jnp.arange(npool, dtype=jnp.int32)
    out_list = []
    dq_list = []
    pick_list = []
    dk_list = []
    dv_list = []
    for block in range(nblock):
        row = shard * nblock + block
        ids = lax.dynamic_index_in_dim(kv_index, row, 0, keepdims=False)
        live = place < lax.dynamic_index_in_dim(count, row, 0, keepdims=False)
        owner = ids // nblock
        slot = jnp.where(owner == shard, ids - shard * nblock, nblock + owner)
        slot = jnp.where(live, slot, 0)
        kb = jnp.take(pool_keys, slot, axis=0)
        vb = jnp.take(pool_values, slot, axis=0)
        qb = q_blocks[block]
        gb = g_blocks[block]
        allowed = live[None, :, None] & (
            (ids[None, :, None] != row) | (tokens[None, None, :] <= tokens[:, None, None])
        )
        score = jnp.einsum("acgd,mncd->cgamn", qb, kb, preferred_element_type=jnp.float32) * scale
        score = jnp.where(allowed[None, None], score, -1e30)
        top = jnp.max(score, axis=(3, 4), keepdims=True)
        expo = jnp.exp(score - top)
        prob = expo / jnp.sum(expo, axis=(3, 4), keepdims=True)
        prob_b = prob.astype(jnp.bfloat16)
        out_b = jnp.einsum(
            "cgamn,mncd->acgd", prob_b, vb, preferred_element_type=jnp.float32
        ).astype(jnp.bfloat16)
        delta = jnp.sum(gb.astype(jnp.float32) * out_b.astype(jnp.float32), axis=-1)
        delta = jnp.transpose(delta, (1, 2, 0))[:, :, :, None, None]
        dprob = jnp.einsum("acgd,mncd->cgamn", gb, vb, preferred_element_type=jnp.float32)
        dscore = (prob * (dprob - delta)).astype(jnp.bfloat16)
        dq = (
            jnp.einsum("cgamn,mncd->acgd", dscore, kb, preferred_element_type=jnp.float32) * scale
        ).astype(jnp.bfloat16)
        dv_slots = jnp.einsum("cgamn,acgd->mncd", prob_b, gb, preferred_element_type=jnp.float32)
        dk_slots = (
            jnp.einsum("cgamn,acgd->mncd", dscore, qb, preferred_element_type=jnp.float32) * scale
        )
        pick_list.append(((slot[:, None] == pool_ids[None, :]) & live[:, None]).astype(jnp.float32))
        dk_list.append(dk_slots.reshape(MAXK, -1))
        dv_list.append(dv_slots.reshape(MAXK, -1))
        out_list.append(out_b.reshape(BLOCK_TOKENS, -1))
        dq_list.append(dq.reshape(BLOCK_TOKENS, -1))
    picks = jnp.concatenate(pick_list, axis=0)
    grad_pool_k = jnp.dot(
        picks.T, jnp.concatenate(dk_list, axis=0), precision=lax.Precision.HIGHEST
    )
    grad_pool_v = jnp.dot(
        picks.T, jnp.concatenate(dv_list, axis=0), precision=lax.Precision.HIGHEST
    )
    attn = jnp.concatenate(out_list, axis=0)[None]
    dquery = jnp.concatenate(dq_list, axis=0)[None]
    own_k = grad_pool_k[:nblock].reshape(rows, width_kv)
    own_v = grad_pool_v[:nblock].reshape(rows, width_kv)
    far_k = grad_pool_k[nblock:].reshape(nseq * BLOCK_TOKENS, width_kv)
    far_v = grad_pool_v[nblock:].reshape(nseq * BLOCK_TOKENS, width_kv)
    mine_k, mine_v = sum_summaries(far_k, far_v)
    dkey = own_k.at[rows - BLOCK_TOKENS :].add(mine_k).astype(jnp.bfloat16)[None]
    dvalue = own_v.at[rows - BLOCK_TOKENS :].add(mine_v).astype(jnp.bfloat16)[None]
    attn_back, dq_back, dk_back, dv_back = (
        lax.all_to_all(attn, "head", split_axis=1, concat_axis=2, tiled=True),
        lax.all_to_all(dquery, "head", split_axis=1, concat_axis=2, tiled=True),
        lax.all_to_all(dkey, "head", split_axis=1, concat_axis=2, tiled=True),
        lax.all_to_all(dvalue, "head", split_axis=1, concat_axis=2, tiled=True),
    )
    return (attn_back, dq_back, dk_back, dv_back)


def solution(mesh):
    in_specs = (
        P("seq", "head", None),
        P("seq", "head", None),
        P("seq", "head", None),
        P("seq", "head", None),
        P(),
        P(),
    )
    out_specs = (
        P("seq", "head", None),
        P("seq", "head", None),
        P("seq", "head", None),
        P("seq", "head", None),
    )
    return jax.shard_map(shards, mesh=mesh, in_specs=in_specs, out_specs=out_specs, check_vma=False)
```

profile of v0, /device:TPU:0, one launch (start us, length us, event | category | flops | bytes accessed | tf_op | source)
XLA Modules:
  0.0 1339.9 jit_solution(11969628956049348054)
XLA Ops:
  7.2 4.6 copy.578
  12.4 7.1 reduce.30
  21.0 4.4 all-to-all-start
  25.5 4.6 copy.583
  30.1 8.0 reduce.31
  44.6 34.5 %copy.588 = bf16[1,512,8192]{1,0,2:T(2,128)(2,1)} copy(bf16[1,512,8192]{2,1,0:T(8,128)(2,1)} %param.12) | data formatting | bytes 16777216 | tf_op args[0]
  79.1 54.8 %reduce.29 = bf16[8192,512]{1,0:T(8,128)(2,1)} reduce(bf16[8192,1,512]{2,1,0:T(2,128)(2,1)} %bitcast.702, bf16[]{:T(256)} %broadcast.1050), dimensions={1}, to_apply=%bitcast.636.reduce_sub_computation | reduce | bytes 16777218
  133.9 10.1 reshape.996
  145.0 7.0 all-to-all-start.2
  157.0 34.6 %copy.646 = bf16[1,512,8192]{1,0,2:T(2,128)(2,1)} copy(bf16[1,512,8192]{2,1,0:T(8,128)(2,1)} %param.15) | data formatting | bytes 16777216 | tf_op args[3]
  191.6 54.8 %reduce.28 = bf16[8192,512]{1,0:T(8,128)(2,1)} reduce(bf16[8192,1,512]{2,1,0:T(2,128)(2,1)} %bitcast.703, bf16[]{:T(256)} %broadcast.1050), dimensions={1}, to_apply=%bitcast.644.reduce_sub_computation | reduce | bytes 16777218
  246.4 10.2 reshape.1004
  266.7 7.2 all-to-all-start.4
  277.4 5.6 concatenate.32
  286.9 18.0 %reshape.997 = bf16[8192,1,512]{2,1,0:T(2,128)(2,1)} reshape(bf16[2,2,1048576]{2,1,0:T(2,128)(2,1)} %all-to-all-done.2) | data formatting | bytes 16777216
  305.0 11.8 copy.966
  316.8 11.7 copy.589
  328.5 9.5 copy.988
  338.0 28.9 %all-to-all-done.4 = bf16[2,2,1048576]{2,1,0:T(2,128)(2,1)} async-done(((bf16[2,2,1048576]{2,1,0:T(2,128)(2,1)}), bf16[2,2,1048576]{2,1,0:T(2,128)(2,1)}, u32[]{:S(2)}, u32[]{:S(2)}) %all-to-all-start.4) | async-done | bytes 8388640 | tf_op jit(solution)/shard_map/all_to_all | solution.py:43
  366.9 18.0 %reshape.1005 = bf16[8192,1,512]{2,1,0:T(2,128)(2,1)} reshape(bf16[2,2,1048576]{2,1,0:T(2,128)(2,1)} %all-to-all-done.4) | data formatting | bytes 16777216
  384.9 11.8 copy.968
  396.7 11.9 copy.647
  408.7 9.6 copy.989
  418.3 5.7 fusion.224
  442.4 6.1 fusion.225
  460.1 5.9 reshape.975
  465.9 4.4 copy.587
  591.6 55.6 %concatenate.35 = f32[24,65536]{1,0:T(8,128)} concatenate(f32[3,65536]{1,0:T(4,128)} %reshape.698, f32[3,65536]{1,0:T(4,128)} %reshape.699, f32[3,65536]{1,0:T(4,128)} %reshape.700, f32[3,65536]{1,0:T(4,128)} %reshape.701, f32[3,65536]{1,0:T(4,128)} %reshape.702, f32[3,65536]{1,0:T(4,128)} %reshape.703, f32[3,65536]{1,0:T(4,128)} %reshape.704, f32[3,65536]{1,0:T(4,128)} %reshape.705), dimensions={0} | concatenate | bytes 12582912 | tf_op jit(solution)/shard_map/concatenate | solution.py:113
  647.2 5.1 fusion.228
  659.8 4.1 multiply_reduce_fusion
  663.9 5.5 fusion.1
  675.2 4.2 multiply_reduce_fusion.1
  679.4 5.4 fusion.3
  694.7 5.8 fusion.5
  706.3 4.1 multiply_reduce_fusion.3
  710.4 5.4 fusion.7
  721.6 4.1 multiply_reduce_fusion.4
  725.7 5.4 fusion.9
  737.0 4.2 multiply_reduce_fusion.5
  741.2 5.4 fusion.11
  755.5 5.4 fusion.13
  769.7 5.8 fusion.15
  781.3 55.0 %concatenate.34 = f32[24,65536]{1,0:T(8,128)} concatenate(f32[3,65536]{1,0:T(4,128)} %reshape.688, f32[3,65536]{1,0:T(4,128)} %reshape.689, f32[3,65536]{1,0:T(4,128)} %reshape.690, f32[3,65536]{1,0:T(4,128)} %reshape.691, f32[3,65536]{1,0:T(4,128)} %reshape.692, f32[3,65536]{1,0:T(4,128)S(1)} %copy-done.36, f32[3,65536]{1,0:T(4,128)S(1)} %copy-done.35, f32[3,65536]{1,0:T(4,128)S(1)} %copy-done.34), dimensions={0} | concatenate | bytes 12582912 | tf_op jit(solution)/shard_map/concatenate | solution.py:110
  836.3 5.1 fusion.227
  905.5 7.1 reduce.35
  920.4 12.6 reduce-scatter.3.cloned.1.call-done
  937.5 8.0 reduce.34
  958.3 20.1 %copy.1210 = bf16[1,1024,4096]{2,0,1:T(2,128)(2,1)} copy(bf16[1,1024,4096]{2,1,0:T(8,128)(2,1)} %bitcast.714) | data formatting | bytes 16777216 | tf_op jit(solution)/shard_map/broadcast_in_dim | solution.py:116
  978.4 52.7 %reduce.33 = bf16[1024,4096]{1,0:T(8,128)(2,1)} reduce(bf16[1024,1,4096]{2,1,0:T(2,128)(2,1)} %bitcast.701, bf16[]{:T(256)} %broadcast.1050), dimensions={1}, to_apply=%bitcast.692.reduce_sub_computation | reduce | bytes 16777218
  1031.0 10.2 reshape.1006
  1042.2 7.2 all-to-all-start.5
  1069.6 43.2 %copy.1211 = bf16[1,1024,4096]{2,0,1:T(2,128)(2,1)} copy(bf16[1,1024,4096]{2,1,0:T(8,128)(2,1)S(1)} %bitcast.715) | data formatting | bytes 16777216 | tf_op jit(solution)/shard_map/broadcast_in_dim | solution.py:115
  1112.8 52.7 %reduce.32 = bf16[1024,4096]{1,0:T(8,128)(2,1)} reduce(bf16[1024,1,4096]{2,1,0:T(2,128)(2,1)} %bitcast.700, bf16[]{:T(256)} %broadcast.1050), dimensions={1}, to_apply=%bitcast.693.reduce_sub_computation | reduce | bytes 16777218
  1165.5 10.2 reshape.1002
  1175.7 7.3 all-to-all-start.3
  1191.1 18.0 %reshape.1007 = bf16[1024,1,4096]{2,1,0:T(2,128)(2,1)} reshape(bf16[2,2,1048576]{2,1,0:T(2,128)(2,1)} %all-to-all-done.5) | data formatting | bytes 16777216
  1209.1 16.8 %copy.969 = bf16[1,1024,4096]{2,1,0:T(8,128)(2,1)} copy(bf16[1,1024,4096]{2,0,1:T(2,128)(2,1)} %bitcast.698) | data formatting | bytes 16777216
  1225.9 12.0 copy.697
  1237.9 11.9 copy.727
  1249.8 24.2 %all-to-all-done.3 = bf16[2,2,1048576]{2,1,0:T(2,128)(2,1)} async-done(((bf16[2,2,1048576]{2,1,0:T(2,128)(2,1)}), bf16[2,2,1048576]{2,1,0:T(2,128)(2,1)}, u32[]{:S(2)}, u32[]{:S(2)}) %all-to-all-start.3) | async-done | bytes 8388640 | tf_op jit(solution)/shard_map/all_to_all | solution.py:125
  1274.0 18.2 %reshape.1003 = bf16[1024,1,4096]{2,1,0:T(2,128)(2,1)} reshape(bf16[2,2,1048576]{2,1,0:T(2,128)(2,1)} %all-to-all-done.3) | data formatting | bytes 16777216
  1292.3 16.8 %copy.967 = bf16[1,1024,4096]{2,1,0:T(8,128)(2,1)} copy(bf16[1,1024,4096]{2,0,1:T(2,128)(2,1)} %bitcast.699) | data formatting | bytes 16777216
  1309.1 12.0 copy.645
  1321.1 11.9 copy.726
  (530 shorter events, 363.7 us)
Async XLA Ops:
  21.0 19.7 %all-to-all-start = ((bf16[2,2,131072]{2,1,0:T(2,128)(2,1)}), bf16[2,2,131072]{2,1,0:T(2,128)(2,1)S(1)}, u32[]{:S(2)}, u32[]{:S(2)}) async-start(bf16[2,2,131072]{2,1,0:T(2,128)(2,1)} %reshape.1000), calls=%async_computation | async-start | bytes 2097152 | tf_op jit(solution)/shard_map/all_to_all | solution.py:42
  40.8 103.3 %all-to-all-start.1 = ((bf16[2,2,131072]{2,1,0:T(2,128)(2,1)}), bf16[2,2,131072]{2,1,0:T(2,128)(2,1)S(1)}, u32[]{:S(2)}, u32[]{:S(2)}) async-start(bf16[2,2,131072]{2,1,0:T(2,128)(2,1)} %reshape.998), calls=%async_computation.1 | async-start | bytes 2097152 | tf_op jit(solution)/shard_map/all_to_all | solution.py:41
  145.0 121.6 %all-to-all-start.2 = ((bf16[2,2,1048576]{2,1,0:T(2,128)(2,1)}), bf16[2,2,1048576]{2,1,0:T(2,128)(2,1)}, u32[]{:S(2)}, u32[]{:S(2)}) async-start(bf16[2,2,1048576]{2,1,0:T(2,128)(2,1)} %reshape.996), calls=%async_computation.2 | async-start | bytes 16777216 | tf_op jit(solution)/shard_map/all_to_all | solution.py:40
  152.0 296.5 %all-gather.5.cloned.1.call-start = ((), (), s32[]{:S(2)}) async-start(), calls=%async_computation.12 | async-start | bytes 2228224 | tf_op jit(solution)/shard_map/all_gather | solution.py:21
  156.2 35.4 %copy-start.32 = (bf16[1,2,512,512]{3,2,1,0:T(8,128)(2,1)}, bf16[1,2,512,512]{3,2,1,0:T(8,128)(2,1)S(1)}, u32[]{:S(2)}) copy-start(bf16[1,2,512,512]{3,2,1,0:T(8,128)(2,1)S(1)} %copy.579) | copy-start | bytes 3145732
  246.4 10.2 copy-start.125
  246.4 10.9 copy-start.110
  266.7 16.3 %copy-start.46 = (bf16[2,2,131072]{2,1,0:T(2,128)(2,1)S(1)}, bf16[2,2,131072]{2,1,0:T(2,128)(2,1)}, u32[]{:S(2)}) copy-start(bf16[2,2,131072]{2,1,0:T(2,128)(2,1)} %copy-done.45) | copy-start | bytes 3145732
  266.7 100.3 %all-to-all-start.4 = ((bf16[2,2,1048576]{2,1,0:T(2,128)(2,1)}), bf16[2,2,1048576]{2,1,0:T(2,128)(2,1)}, u32[]{:S(2)}, u32[]{:S(2)}) async-start(bf16[2,2,1048576]{2,1,0:T(2,128)(2,1)} %reshape.1004), calls=%async_computation.4 | async-start | bytes 16777216 | tf_op jit(solution)/shard_map/all_to_all | solution.py:43
  273.9 182.4 %all-gather.7.cloned.1.call-start = ((), (), s32[]{:S(2)}) async-start(), calls=%async_computation.13 | async-start | bytes 2228224 | tf_op jit(solution)/shard_map/all_gather | solution.py:20
  284.8 20.2 %copy-start.33 = (bf16[1,2,512,512]{3,2,1,0:T(8,128)(2,1)}, bf16[1,2,512,512]{3,2,1,0:T(8,128)(2,1)S(1)}, u32[]{:S(2)}) copy-start(bf16[1,2,512,512]{3,2,1,0:T(8,128)(2,1)S(1)} %copy.584) | copy-start | bytes 3145732
  285.5 617.4 %reduce-scatter.5.cloned.1.call-start = ((), (), s32[]{:S(2)}) async-start(), calls=%async_computation.11 | async-start | bytes 2228224 | tf_op jit(solution)/shard_map/reduce_scatter | solution.py:30
  506.6 5.4 copy-start.95
  524.7 4.7 copy-start.27
  524.7 4.7 copy-start.91
  577.1 5.3 copy-start.80
  591.6 55.6 %copy-start.126 = (pred[24,24]{1,0:T(8,128)(4,1)S(1)}, pred[24,24]{1,0:T(8,128)(4,1)}, u32[]{:S(2)}) copy-start(pred[24,24]{1,0:T(8,128)(4,1)} %concatenate.32) | copy-start | bytes 1732
  656.5 7.3 copy-start.96
  656.6 7.3 copy-start.109
  656.6 7.3 copy-start.124
  659.8 273.2 %reduce-scatter.3.cloned.1.call-start = ((), (), s32[]{:S(2)}) async-start(), calls=%async_computation.10 | async-start | bytes 2228224 | tf_op jit(solution)/shard_map/reduce_scatter | solution.py:27
  663.9 5.5 copy-start.31
  669.4 10.0 copy-start.94
  669.5 10.0 copy-start.107
  669.5 9.9 copy-start.122
  679.4 5.4 copy-start.30
  684.9 9.8 copy-start.92
  684.9 9.8 copy-start.105
  684.9 9.8 copy-start.120
  694.7 5.9 copy-start.28
  700.6 9.8 copy-start.90
  700.6 9.8 copy-start.103
  700.6 9.8 copy-start.118
  710.4 5.4 copy-start.26
  715.9 9.8 copy-start.88
  715.9 9.8 copy-start.101
  715.9 9.8 copy-start.116
  725.7 5.4 copy-start.24
  731.1 10.1 copy-start.86
  731.1 10.1 copy-start.99
  731.1 10.1 copy-start.114
  741.2 5.4 copy-start.22
  746.6 8.8 copy-start.84
  746.6 8.8 copy-start.112
  755.5 5.4 copy-start.20
  760.9 5.7 copy-start.11
  760.9 8.8 copy-start.81
  769.7 5.8 copy-start.18
  775.5 5.7 copy-start.34
  775.6 5.7 copy-start.35
  775.6 5.7 copy-start.36
  781.3 55.0 %copy-start.127 = (pred[24,24]{1,0:T(8,128)(4,1)S(1)}, pred[24,24]{1,0:T(8,128)(4,1)}, u32[]{:S(2)}) copy-start(pred[24,24]{1,0:T(8,128)(4,1)} %concatenate.32) | copy-start | bytes 1732
  844.4 10.5 copy-start.55
  846.4 12.0 copy-start.57
  850.1 12.2 copy-start.59
  851.6 10.7 copy-start.135
  858.5 5.6 copy-start.61
  858.5 5.6 copy-start.137
  914.2 33.9 %all-to-all-start.7 = ((bf16[2,2,131072]{2,1,0:T(2,128)(2,1)}), bf16[2,2,131072]{2,1,0:T(2,128)(2,1)S(1)}, u32[]{:S(2)}, u32[]{:S(2)}) async-start(bf16[2,2,131072]{2,1,0:T(2,128)(2,1)} %reshape.1010), calls=%async_computation.9 | async-start | bytes 2097152 | tf_op jit(solution)/shard_map/all_to_all | solution.py:128
  918.0 34.1 %copy-start.53 = (bf16[3,128,4,128,1]{3,1,2,0,4:T(8,128)(2,1)S(1)}, bf16[3,128,4,128,1]{3,1,2,0,4:T(8,128)(2,1)}, u32[]{:S(2)}) copy-start(bf16[3,128,4,128,1]{3,1,2,0,4:T(8,128)(2,1)} %copy-done.52) | copy-start | bytes 1179652
  948.1 93.1 %all-to-all-start.6 = ((bf16[2,2,131072]{2,1,0:T(2,128)(2,1)}), bf16[2,2,131072]{2,1,0:T(2,128)(2,1)S(1)}, u32[]{:S(2)}, u32[]{:S(2)}) async-start(bf16[2,2,131072]{2,1,0:T(2,128)(2,1)} %reshape.1008), calls=%async_computation.7 | async-start | bytes 2097152 | tf_op jit(solution)/shard_map/all_to_all | solution.py:127
  1041.2 8.2 copy-start.97
  1042.2 133.5 %all-to-all-start.5 = ((bf16[2,2,1048576]{2,1,0:T(2,128)(2,1)}), bf16[2,2,1048576]{2,1,0:T(2,128)(2,1)}, u32[]{:S(2)}, u32[]{:S(2)}) async-start(bf16[2,2,1048576]{2,1,0:T(2,128)(2,1)} %reshape.1006), calls=%async_computation.5 | async-start | bytes 16777216 | tf_op jit(solution)/shard_map/all_to_all | solution.py:126
  1175.7 98.3 %all-to-all-start.3 = ((bf16[2,2,1048576]{2,1,0:T(2,128)(2,1)}), bf16[2,2,1048576]{2,1,0:T(2,128)(2,1)}, u32[]{:S(2)}, u32[]{:S(2)}) async-start(bf16[2,2,1048576]{2,1,0:T(2,128)(2,1)} %reshape.1002), calls=%async_computation.3 | async-start | bytes 16777216 | tf_op jit(solution)/shard_map/all_to_all | solution.py:125
  (91 other events, 260.9 us)
Sparse Core Ops, SparseCore 0:
  157.1 43.8 all-gather.4
  285.6 43.7 all-gather.6
  659.9 62.3 reduce-scatter.4
  870.5 62.3 reduce-scatter.2
where the time goes:
time: 1360 us; the launch traced here: 1340 us
  local copies, waits for them, and re-layouts  775 us (57%)
  other arithmetic  301 us (22%)
  matrix products  137 us (10%)
  waiting for transfers between devices  65.8 us (5%)
  starting transfers between devices  45.5 us (3%)
  between operations  16.3 us (1%)
    unnamed x343, local copies, waits for them, and re-layouts  366 us
    unnamed x8, other arithmetic  245 us
    concatenate x1, local copies, waits for them, and re-layouts, shards(): jnp.concatenate(dv_list, axis=0)  55.6 us
    concatenate x1, local copies, waits for them, and re-layouts, shards(): jnp.concatenate(dk_list, axis=0)  55 us
    dot_general x8, matrix products, shards(): jnp.einsum('acgd,mncd->cgamn', gb, vb, preferred_element_type=jnp.float32)  44.2 us
    broadcast_in_dim x1, local copies, waits for them, and re-layouts, shards(): attn = jnp.concatenate(out_list, axis=0)[None]  43.2 us
    dot_general x8, matrix products, shards(): jnp.einsum('cgamn,mncd->acgd', prob_b, vb, preferred_element_type=jnp.flo...  30.9 us
    all_to_all x1, waiting for transfers between devices, shards(): lax.all_to_all(output_gradient, 'head', split_axis=2, concat_axis=1, tile...  28.9 us
  transfers between devices with their start and end apart: 12, of which 3 were waited for; matrix products, arithmetic and copies ran while one was open for 69% of the time, Pallas kernels for 0%

commit v1 on v0

v1 whole, which is shorter than its diff:
```python
import functools
import math

import jax
import jax.numpy as jnp
from jax import lax
from jax.experimental import pallas as pl
from jax.experimental.pallas import tpu as pltpu
from jax.sharding import PartitionSpec as P

HEAD = 128
TOK = 128
MAXK = 3
DEAD = -1e30
CHUNKS = 1
SPLIT = 4


def attend(
    nb, nseq, query_group,
    meta,
    q_ref, g_ref, k_ref, v_ref, near_ref, tail_ref, *rest,
):
    out_ref, dq_ref, dk_ref, dv_ref, dnear_ref, dtail_ref, x_ref, pd_ref, far_ref = rest[-9:]
    f32, bf16 = jnp.float32, jnp.bfloat16
    scale = 1.0 / math.sqrt(HEAD)
    factor = scale * math.log2(math.e)
    zero = jnp.zeros((TOK, HEAD), bf16)
    causal = (
        lax.broadcasted_iota(jnp.int32, (TOK, TOK), 0)
        <= lax.broadcasted_iota(jnp.int32, (TOK, TOK), 1)
    )
    bias = jnp.where(causal, 0.0, DEAD).astype(f32)
    bias = jnp.concatenate([bias] * SPLIT, axis=1)
    prev_is_tail = meta[3 * nb] > 0
    prev_slot = pl.multiple_of(meta[3 * nb + 1] * TOK, TOK)
    dtail_ref[...] = jnp.zeros_like(dtail_ref)
    dnear_ref[...] = jnp.zeros_like(dnear_ref)

    for r in range(nb):
        rows = slice(r * TOK, (r + 1) * TOK)
        live = [None, meta[3 * r] > 0, meta[3 * r + 1] > 0]
        slot = pl.multiple_of(meta[3 * r + 2] * TOK, TOK)
        kv = [(k_ref[rows, :], v_ref[rows, :])]
        if r:
            before = slice((r - 1) * TOK, r * TOK)
            kv.append((k_ref[before, :], v_ref[before, :]))
        else:
            tail = tail_ref[pl.ds(prev_slot, TOK), :]
            pick = jnp.where(prev_is_tail, tail.astype(f32), near_ref[...].astype(f32)).astype(bf16)
            kv.append((pick[:, :HEAD], pick[:, HEAD:]))
        tail = tail_ref[pl.ds(slot, TOK), :]
        kv.append((tail[:, :HEAD], tail[:, HEAD:]))
        a = jnp.concatenate(
            [
                part
                for k, v in kv
                for part in (
                    jnp.concatenate([k, zero], axis=1),
                    jnp.concatenate([zero, v], axis=1),
                )
            ],
            axis=0,
        )
        b = jnp.concatenate(
            [
                jnp.concatenate(
                    [part for k, v in kv for part in (v.T, zero)], axis=1
                ),
                jnp.concatenate(
                    [part for k, v in kv for part in (zero, k.T)], axis=1
                ),
            ],
            axis=0,
        )
        for c in range(query_group // SPLIT):
            span = SPLIT * TOK
            at = slice(c * span, (c + 1) * span)
            for h in range(SPLIT):
                lanes = slice((c * SPLIT + h) * HEAD, (c * SPLIT + h + 1) * HEAD)
                there = slice((c * SPLIT + h) * TOK, (c * SPLIT + h + 1) * TOK)
                x_ref[there, :HEAD] = q_ref[rows, lanes]
                x_ref[there, HEAD:] = g_ref[rows, lanes]
            st = lax.dot_general(
                a, x_ref[at, :], (((1,), (1,)), ((), ())), preferred_element_type=f32
            )
            s = [st[2 * j * TOK : (2 * j + 1) * TOK] for j in range(MAXK)]
            dp = [st[(2 * j + 1) * TOK : (2 * j + 2) * TOK] for j in range(MAXK)]
            s[0] = s[0] + bias
            tops = [jnp.max(x, axis=0, keepdims=True) for x in s]
            top = tops[0]
            for j in (1, 2):
                top = jnp.maximum(top, jnp.where(live[j], tops[j], DEAD))
            p = []
            for j in range(MAXK):
                base = top if j == 0 else jnp.where(live[j], top, -DEAD)
                p.append(jnp.exp2((s[j] - base) * factor))
            total = sum(jnp.sum(x, axis=0, keepdims=True) for x in p)
            inv = 1.0 / total
            delta = sum(jnp.sum(x * y, axis=0, keepdims=True) for x, y in zip(p, dp)) * inv
            for j in range(MAXK):
                prob = p[j] * inv
                pd_ref[2 * j * TOK : (2 * j + 1) * TOK, at] = prob.astype(bf16)
                pd_ref[(2 * j + 1) * TOK : (2 * j + 2) * TOK, at] = (
                    prob * (dp[j] - delta)
                ).astype(bf16)
            ot = jnp.dot(b, pd_ref[:, at], preferred_element_type=f32)
            for h in range(SPLIT):
                lanes = slice((c * SPLIT + h) * HEAD, (c * SPLIT + h + 1) * HEAD)
                piece = ot[:, h * TOK : (h + 1) * TOK]
                out_ref[rows, lanes] = piece[:HEAD].T.astype(bf16)
                dq_ref[rows, lanes] = (piece[HEAD:].T * scale).astype(bf16)
        dkv = jnp.dot(pd_ref[...], x_ref[...], preferred_element_type=f32)

        def grads(j):
            return (
                dkv[(2 * j + 1) * TOK : (2 * j + 2) * TOK, :HEAD] * scale,
                dkv[2 * j * TOK : (2 * j + 1) * TOK, HEAD:],
            )

        dk, dv = grads(0)
        dk_ref[rows, :] = dk
        dv_ref[rows, :] = dv
        dk, dv = grads(1)
        if r:
            dk_ref[before, :] += dk
            dv_ref[before, :] += dv
        else:
            far_ref[nb, :, :HEAD] = dk
            far_ref[nb, :, HEAD:] = dv
        dk, dv = grads(2)
        far_ref[r, :, :HEAD] = dk
        far_ref[r, :, HEAD:] = dv

    first = far_ref[nb]
    first_far = jnp.logical_and(prev_is_tail, meta[0] > 0)

    @pl.when(jnp.logical_not(prev_is_tail))
    def _():
        dnear_ref[...] = first.astype(bf16)

    @pl.when(first_far)
    def _():
        dtail_ref[pl.ds(prev_slot, TOK), :] = first.astype(bf16)

    for r in range(nb):
        @pl.when(meta[3 * r + 1] > 0)
        def _(r=r):
            mine = meta[3 * r + 2]
            sum_ = far_ref[r]
            same = jnp.logical_and(first_far, meta[3 * nb + 1] == mine)
            sum_ = sum_ + jnp.where(same, far_ref[nb], 0.0)
            for e in range(r):
                same = jnp.logical_and(meta[3 * e + 1] > 0, meta[3 * e + 2] == mine)
                sum_ = sum_ + jnp.where(same, far_ref[e], 0.0)
            dtail_ref[pl.ds(pl.multiple_of(mine * TOK, TOK), TOK), :] = sum_.astype(bf16)


def call(nb, nseq, width, first, groups, query_group, meta, q, g, k, v, near, tails, earlier):
    rows = nb * TOK
    wide = query_group * HEAD
    width_kv = k.shape[1]

    def at(i, meta):
        return (0, i)

    def global_at(i, meta):
        return (0, first + i)

    big = pl.BlockSpec((rows, wide), global_at)
    own = pl.BlockSpec((rows, HEAD), global_at)
    in_specs = [
        big, big, own, own,
        pl.BlockSpec((TOK, 2 * HEAD), at),
        pl.BlockSpec((nseq * TOK, 2 * HEAD), at),
    ]
    operands = [q, g, k, v, near, tails]
    aliases = {}
    for i, e in enumerate(earlier):
        aliases[1 + len(operands)] = i
        operands.append(e)
        in_specs.append(pl.BlockSpec(memory_space=pl.ANY))
    bf16, f32 = jnp.bfloat16, jnp.float32
    sds = jax.ShapeDtypeStruct
    flops = 2 * rows * wide * MAXK * TOK * 6 * groups
    return pl.pallas_call(
        functools.partial(attend, nb, nseq, query_group),
        out_shape=(
            sds((rows, width), bf16), sds((rows, width), bf16),
            sds((rows, width_kv), f32), sds((rows, width_kv), f32),
            sds((TOK, groups * 2 * HEAD), bf16),
            sds((nseq * TOK, groups * 2 * HEAD), bf16),
        ),
        grid_spec=pltpu.PrefetchScalarGridSpec(
            num_scalar_prefetch=1,
            grid=(groups,),
            in_specs=in_specs,
            out_specs=[
                big, big, own, own,
                pl.BlockSpec((TOK, 2 * HEAD), at),
                pl.BlockSpec((nseq * TOK, 2 * HEAD), at),
            ],
            scratch_shapes=[
                pltpu.VMEM((query_group * TOK, 2 * HEAD), bf16),
                pltpu.VMEM((2 * MAXK * TOK, query_group * TOK), bf16),
                pltpu.VMEM((nb + 1, TOK, 2 * HEAD), f32),
            ],
        ),
        input_output_aliases=aliases,
        compiler_params=pltpu.CompilerParams(
            dimension_semantics=("arbitrary",), vmem_limit_bytes=48 * 1024 * 1024
        ),
        cost_estimate=pl.CostEstimate(
            flops=flops, bytes_accessed=4 * 2 * rows * wide * groups, transcendentals=0
        ),
        name="attend",
    )(meta, *operands)


def shards(query, key, value, output_gradient, kv_index, count):
    nseq, nhead = lax.axis_size("seq"), lax.axis_size("head")
    shard, part = lax.axis_index("seq"), lax.axis_index("head")
    rows, width = query.shape[1:]
    width_kv = key.shape[2]
    nb = rows // TOK
    ngroup = width_kv // HEAD
    query_group = width // width_kv
    blocks = nb * nhead
    row0 = shard * blocks + part * nb
    ids = lax.dynamic_slice_in_dim(kv_index, row0, nb, 0)
    n = lax.dynamic_slice_in_dim(count, row0, nb, 0)
    row = row0 + jnp.arange(nb, dtype=jnp.int32)
    prev = (n >= 2) & (ids[:, 1] == row - 1)
    strided = (n == 3) | ((n == 2) & ~prev)
    owner = jnp.where(n == 3, ids[:, 2], ids[:, 1]) // blocks
    owner = jnp.where(strided, owner, 0)
    per_row = jnp.stack([prev.astype(jnp.int32), strided.astype(jnp.int32), owner], axis=1)
    ends = jnp.stack([(part == 0).astype(jnp.int32), jnp.maximum(shard - 1, 0)])
    meta = jnp.concatenate([per_row.reshape(-1), ends]).astype(jnp.int32)

    q, g, k, v = query[0], output_gradient[0], key[0], value[0]
    last = jnp.stack(
        [k[rows - TOK :].reshape(TOK, ngroup, HEAD), v[rows - TOK :].reshape(TOK, ngroup, HEAD)],
        axis=2,
    ).reshape(TOK, 2 * width_kv)
    step = ngroup // CHUNKS
    cols = step * 2 * HEAD
    up = [(i, i + 1) for i in range(nhead - 1)]
    pair = [(0, 1), (1, 0)]
    if nhead == 2:
        near = lax.ppermute(last, "head", pair)
        tail = jnp.where(part == 1, last, near)
    else:
        near = lax.ppermute(last, "head", up)
        tail = lax.all_gather(last, "head", axis=0)[nhead - 1]
    gathered = [
        lax.all_gather(tail[:, c * cols : (c + 1) * cols], "seq", axis=0, tiled=True)
        for c in range(CHUNKS)
    ]
    earlier = ()
    tail_grads, near_grads = [], []
    for c in range(CHUNKS):
        *earlier, near_grad, tail_grad = call(
            nb, nseq, width, c * step, step, query_group, meta, q, g, k, v,
            near[:, c * cols : (c + 1) * cols], gathered[c], earlier,
        )
        near_grads.append(near_grad)
        tail_grads.append(
            lax.psum_scatter(tail_grad, "seq", scatter_dimension=0, tiled=True)
        )
    attn, dquery, dkey, dvalue = earlier
    near_grad = jnp.concatenate(near_grads, axis=1)
    tail_grad = jnp.concatenate(tail_grads, axis=1)
    if nhead == 2:
        other = lax.ppermute(jnp.where(part == 0, tail_grad, near_grad), "head", pair)
        add = other.astype(jnp.float32) + jnp.where(part == 1, tail_grad.astype(jnp.float32), 0.0)
    else:
        total = lax.psum(tail_grad, "head").astype(jnp.float32)
        other = lax.ppermute(near_grad, "head", [(j, i) for i, j in up])
        add = other.astype(jnp.float32) + jnp.where(part == nhead - 1, total, 0.0)
    add = add.reshape(TOK, ngroup, 2, HEAD)
    dkey = dkey.at[rows - TOK :].add(add[:, :, 0].reshape(TOK, width_kv))
    dvalue = dvalue.at[rows - TOK :].add(add[:, :, 1].reshape(TOK, width_kv))
    return (
        attn[None], dquery[None],
        dkey.astype(jnp.bfloat16)[None], dvalue.astype(jnp.bfloat16)[None],
    )


def solution(mesh):
    spec = P("seq", "head", None)
    return jax.shard_map(
        shards,
        mesh=mesh,
        in_specs=(spec,) * 4 + (P(), P()),
        out_specs=(spec,) * 4,
        check_vma=False,
    )
```

time: 1360 us -> 305 us (0.22); the launches traced: 1340 us -> 305 us
  local copies, waits for them, and re-layouts: 775 us -> 11.9 us
  other arithmetic: 301 us -> 7.35 us
  waiting for transfers between devices: 65.8 us -> 205 us
  matrix products: 137 us -> 0 us
  Pallas kernels: 0 us -> 63.2 us
  starting transfers between devices: 45.5 us -> 3.6 us
    unnamed x343 -> x12, local copies, waits for them, and re-layouts: 366 us -> 2.48 us
    unnamed x8 -> x0, other arithmetic: 245 us -> none
    dot_general x50 -> x0, matrix products: 137 us -> none  [the longest x8 44.2 us: shards(): jnp.einsum('acgd,mncd->cgamn', gb, vb, preferred_element_type=jnp.float32)]
    concatenate x5 -> x0, local copies, waits for them, and re-layouts: 117 us -> none  [the longest x1 55.6 us: shards(): jnp.concatenate(dv_list, axis=0)]
    reduce_scatter x2 -> x1, waiting for transfers between devices: 12.6 us -> 103 us  [shards(): lax.psum_scatter(tail_grad, 'seq', scatter_dimension=0, tiled=True)]
    reshape x38 -> x3, local copies, waits for them, and re-layouts: 85.3 us -> 2.33 us  [the longest x1 1.86 us: shards(): add = add.reshape(TOK, ngroup, 2, HEAD)]
    all_gather x2 -> x1, waiting for transfers between devices: 0.04 us -> 75.8 us  [shards(): lax.all_gather(tail[:, c * cols:(c + 1) * cols], 'seq', axis=0, tiled=True)]
    broadcast_in_dim x4 -> x0, local copies, waits for them, and re-layouts: 67.7 us -> none  [the longest x1 43.2 us: shards(): attn = jnp.concatenate(out_list, axis=0)[None]]
  transfers between devices with their start and end apart: 12 -> 4, of which waited for: 3 -> 4; matrix products, arithmetic and copies ran while one was open for 69% -> 0% of each run, Pallas kernels for 0% -> 0%
where the time goes in v1:
time: 305 us
  waiting for transfers between devices  205 us (67%)
  Pallas kernels  63.2 us (21%)
  between operations  14.2 us (5%)
  local copies, waits for them, and re-layouts  11.9 us (4%)
  other arithmetic  7.35 us (2%)
  starting transfers between devices  3.6 us (1%)
    reduce_scatter x1, waiting for transfers between devices, shards(): lax.psum_scatter(tail_grad, 'seq', scatter_dimension=0, tiled=True)  103 us
    all_gather x1, waiting for transfers between devices, shards(): lax.all_gather(tail[:, c * cols:(c + 1) * cols], 'seq', axis=0, tiled=True)  75.8 us
    pallas_call x1, Pallas kernels, call(): pl.pallas_call(functools.partial(attend, nb, nseq, query_group), out_shap...  63.2 us
    ppermute x1, waiting for transfers between devices, shards(): lax.ppermute(jnp.where(part == 0, tail_grad, near_grad), 'head', pair)  13.3 us
    ppermute x1, waiting for transfers between devices, shards(): near = lax.ppermute(last, 'head', pair)  11.9 us
  transfers between devices with their start and end apart: 4, of which 4 were waited for; matrix products, arithmetic and copies ran while one was open for 0% of the time, Pallas kernels for 0%

profile of v1, /device:TPU:0, one launch (start us, length us, event | category | flops | bytes accessed | tf_op | source)
XLA Modules:
  0.0 304.8 jit_solution(5203379969157153350)
XLA Ops:
  7.2 0.0 copy-start
  7.2 0.0 all-gather.2.cloned.1.call-start
  7.2 1.0 slice.61
  8.2 0.2 stack_reshape.8
  8.4 1.0 slice.62
  9.4 0.2 stack_reshape.9
  9.7 0.0 copy-start.5
  9.7 1.2 pad_maximum_fusion
  10.9 0.4 reshape.75
  11.3 3.0 collective-permute-start
  14.3 11.9 %collective-permute-done.near_ref = bf16[128,2048]{1,0:T(8,128)(2,1)S(1)} collective-permute-done((bf16[128,2048]{1,0:T(8,128)(2,1)S(1)}, bf16[128,2048]{1,0:T(8,128)(2,1)S(1)}, u32[]{:S(2)}, u32[]{:S(2)}) %collective-permute-start) | collective-permute-done | bytes 524320 | tf_op jit(solution)/shard_map/ppermute | solution.py:251
  26.2 0.8 broadcast_select_fusion.1
  27.1 0.0 all-gather.2.cloned.1.call-update
  27.1 0.0 reduce-scatter.2.cloned.1.call-start
  27.2 0.0 copy-done
  27.2 0.1 constant_dynamic-slice_fusion
  27.3 0.0 copy-done.5
  27.3 0.1 convert_bitcast_fusion.3
  27.3 0.1 convert_bitcast_fusion.2
  27.4 0.1 select_bitcast_fusion
  27.5 0.1 copy.10
  27.6 0.1 reshape.74
  27.7 0.1 pad_add_fusion.1.meta
  27.8 75.8 %all-gather.2.cloned.1.call-done.tail_ref = bf16[2048,2048]{1,0:T(8,128)(2,1)} async-done(((bf16[128,2048]{1,0:T(8,128)(2,1)}), bf16[2048,2048]{1,0:T(8,128)(2,1)}) %all-gather.2.cloned.1.call-update) | async-done | bytes 8388624 | tf_op jit(solution)/shard_map/all_gather | solution.py:257
  103.6 0.0 copy-start.2
  103.6 1.2 copy-done.2
  104.8 0.0 copy-start.3
  104.9 1.2 copy-done.3
  106.1 63.2 %attend.1 = (bf16[512,8192]{1,0:T(8,128)(2,1)}, bf16[512,8192]{1,0:T(8,128)(2,1)}, f32[512,1024]{1,0:T(8,128)S(1)}, f32[512,1024]{1,0:T(8,128)}, bf16[128,2048]{...) custom-call(s32[14]{0:T(128)S(1)} %pad_add_fusion.1.meta, bf16[512,8192]{1,0:T(8,128)(2,1)} %bitcast.42, ...), custom_call_target="tpu_custom_call" | custom-call | flops 19327352832 | bytes 33554432 | tf_op jit(solution)/shard_map/attend/pallas_call | solution.py:186
  169.3 0.0 reduce-scatter.2.cloned.1.call-update
  169.3 103.5 %reduce-scatter.2.cloned.1.call-done = bf16[128,2048]{1,0:T(8,128)(2,1)} async-done(((bf16[2048,2048]{1,0:T(8,128)(2,1)}), bf16[128,2048]{1,0:T(8,128)(2,1)}) %reduce-scatter.2.cloned.1.call-update) | async-done | bytes 524304 | tf_op jit(solution)/shard_map/reduce_scatter | solution.py:269
  272.8 1.1 broadcast_select_fusion
  273.9 0.5 collective-permute-start.1
  274.4 13.3 %collective-permute-done.1 = bf16[128,2048]{1,0:T(8,128)(2,1)S(1)} collective-permute-done((bf16[128,2048]{1,0:T(8,128)(2,1)S(1)}, bf16[128,2048]{1,0:T(8,128)(2,1)S(1)}, u32[]{:S(2)}, u32[]{:S(2)}) %collective-permute-start.1) | collective-permute-done | bytes 524320 | tf_op jit(solution)/shard_map/ppermute | solution.py:275
  287.7 1.2 select_add_fusion
  288.9 1.9 reshape.76
  290.7 0.0 copy-start.4
  290.7 4.5 %slice_reduce_fusion = (f32[128,8,128]{2,1,0:T(8,128)S(1)}, f32[128,8,128]{2,1,0:T(8,128)S(1)}) fusion(f32[128,8,2,128]{3,2,1,0:T(2,128)} %reshape.76), kind=kLoop, calls=%fused_computation.7 | loop fusion | bytes 2097152 | tf_op jit(solution)/shard_map/slice | solution.py:283
  295.3 0.0 copy-done.4
  295.3 0.4 fusion
  295.7 0.0 copy-start.1
  295.7 1.1 convert_bitcast_fusion
  296.8 1.1 convert_bitcast_fusion.1
  298.0 0.0 copy-done.1
  (1 shorter events, 0.0 us)
Async XLA Ops:
  7.2 20.0 %copy-start = (s32[128,3]{0,1:T(4,128)S(1)}, s32[128,3]{0,1:T(4,128)}, u32[]{:S(2)}) copy-start(s32[128,3]{0,1:T(4,128)} %param.14) | copy-start | bytes 4612
  7.2 96.4 %all-gather.2.cloned.1.call-start = ((), (), s32[]{:S(2)}) async-start(), calls=%async_computation.1 | async-start | bytes 8912896 | tf_op jit(solution)/shard_map/all_gather | solution.py:257
  9.7 17.6 %copy-start.5 = (s32[128]{0:T(128)S(1)}, s32[128]{0:T(128)}, u32[]{:S(2)}) copy-start(s32[128]{0:T(128)} %param.15) | copy-start | bytes 1540
  11.3 15.0 %collective-permute-start = (bf16[128,2048]{1,0:T(8,128)(2,1)S(1)}, bf16[128,2048]{1,0:T(8,128)(2,1)S(1)}, u32[]{:S(2)}, u32[]{:S(2)}) collective-permute-start(bf16[128,2048]{1,0:T(8,128)(2,1)S(1)} %reshape.75), channel_id=1, source_target_pairs={{0,16},{16,0},{1,17},{17,1},{2,18},{18,2},{3,19},{19,3},{4,20},{20... | collective-permute-start | bytes 1572872 | tf_op jit(solution)/shard_map/ppermute | solution.py:251
  27.1 245.7 %reduce-scatter.2.cloned.1.call-start = ((), (), s32[]{:S(2)}) async-start(), calls=%async_computation.2 | async-start | bytes 8912896 | tf_op jit(solution)/shard_map/reduce_scatter | solution.py:269
  103.6 1.2 copy-start.2
  104.8 1.2 copy-start.3
  273.9 13.8 %collective-permute-start.1 = (bf16[128,2048]{1,0:T(8,128)(2,1)S(1)}, bf16[128,2048]{1,0:T(8,128)(2,1)S(1)}, u32[]{:S(2)}, u32[]{:S(2)}) collective-permute-start(bf16[128,2048]{1,0:T(8,128)(2,1)S(1)} %broadcast_select_fusion), channel_id=1, source_target_pairs={{0,16},{16,0},{1,17},{17,1},{2,18},{18,2},{3,19},{19,3},{4,20},{20... | collective-permute-start | bytes 1572872 | tf_op jit(solution)/shard_map/ppermute | solution.py:275
  290.7 4.5 %copy-start.4 = (f32[512,1024]{1,0:T(8,128)S(1)}, f32[512,1024]{1,0:T(8,128)}, u32[]{:S(2)}) copy-start(f32[512,1024]{1,0:T(8,128)} %get-tuple-element.39) | copy-start | bytes 6291460
  295.7 2.3 copy-start.1
Sparse Core Ops, SparseCore 0:
  27.2 76.3 all-gather.1
  169.4 103.3 reduce-scatter.1

commit v2 on v1

--- a/solution.py
+++ b/solution.py
@@ -217,6 +217,169 @@
     )(meta, *operands)
 
 
+PIECES = 2
+
+
+def ring_place(n):
+    across = n // 8
+    me = lax.axis_index("seq")
+    x, z = me // 2 % across, me // (2 * across)
+    place = (x * 4 + z + (x % 2) * (3 - 2 * z)) * 2 + me % 2
+
+    def index(p):
+        p = (p + n) % n
+        x, z = p // 8, p // 2 % 4
+        z = z + (x % 2) * (3 - 2 * z)
+        return z * (2 * across) + x * 2 + p % 2
+
+    return me, place, index
+
+
+def greet(left, right):
+    barrier = pltpu.get_barrier_semaphore()
+    for neighbour in (left, right):
+        pl.semaphore_signal(
+            barrier, inc=1, device_id={"seq": neighbour}, device_id_type=pl.DeviceIdType.MESH
+        )
+    pl.semaphore_wait(barrier, 2)
+
+
+LANES = [(way, piece) for piece in range(PIECES) for way in range(2)]
+
+
+def gather_ring(n, half, tail_ref, out_ref, send_sem, recv_sem, own_sem):
+    me, place, index = ring_place(n)
+    right, left = index(place + 1), index(place - 1)
+    size = TOK // PIECES
+    greet(left, right)
+
+    def window(t, way, piece):
+        owner = index(place - t) if way == 0 else index(place + t)
+        start = pl.multiple_of(owner * TOK + piece * size, size)
+        return out_ref.at[pl.ds(start, size), pl.ds(way * half, half)]
+
+    def copy(t, sem, way, piece, src=None):
+        there = window(t, way, piece)
+        return pltpu.make_async_remote_copy(
+            src_ref=there if src is None else src,
+            dst_ref=there,
+            send_sem=send_sem.at[way, piece, sem],
+            recv_sem=recv_sem.at[way, piece, sem],
+            device_id={"seq": right if way == 0 else left},
+            device_id_type=pl.DeviceIdType.MESH,
+        )
+
+    for way, piece in LANES:
+        src = tail_ref.at[pl.ds(piece * size, size), pl.ds(way * half, half)]
+        copy(0, 0, way, piece, src).start()
+    own = pltpu.make_async_copy(
+        tail_ref, out_ref.at[pl.ds(pl.multiple_of(me * TOK, TOK), TOK), :], own_sem
+    )
+    own.start()
+
+    def step(t, carry):
+        for way, piece in LANES:
+            copy(t, t - 1, way, piece).wait_recv()
+            copy(t, t, way, piece).start()
+        return carry
+
+    lax.fori_loop(1, n - 1, step, 0)
+    for way, piece in LANES:
+        copy(n - 1, n - 2, way, piece).wait_recv()
+    own.wait()
+
+    def finish(t, carry):
+        for way, piece in LANES:
+            copy(t, t, way, piece).wait_send()
+        return carry
+
+    lax.fori_loop(0, n - 1, finish, 0)
+
+
+def reduce_ring(n, half, term_ref, sum_ref, slots, send_sem, recv_sem):
+    me, place, index = ring_place(n)
+    right, left = index(place + 1), index(place - 1)
+    size = TOK // PIECES
+    greet(left, right)
+
+    def term(t, way, piece):
+        owner = index(place - 1 - t) if way == 0 else index(place + 1 + t)
+        start = pl.multiple_of(owner * TOK + piece * size, size)
+        return term_ref.at[pl.ds(start, size), pl.ds(way * half, half)]
+
+    def slot(t, way, piece):
+        return slots.at[t, way, pl.ds(piece * size, size), :]
+
+    def copy(t, way, piece, src):
+        return pltpu.make_async_remote_copy(
+            src_ref=src,
+            dst_ref=slot(t, way, piece),
+            send_sem=send_sem.at[way, piece, t],
+            recv_sem=recv_sem.at[way, piece, t],
+            device_id={"seq": right if way == 0 else left},
+            device_id_type=pl.DeviceIdType.MESH,
+        )
+
+    for way, piece in LANES:
+        copy(0, way, piece, term(0, way, piece)).start()
+
+    def total(t, way, piece):
+        held = slot(t - 1, way, piece)
+        copy(t - 1, way, piece, held).wait_recv()
+        return held[...].astype(jnp.float32) + term(t, way, piece)[...].astype(jnp.float32)
+
+    def step(t, carry):
+        for way, piece in LANES:
+            value = total(t, way, piece)
+            held = slot(t - 1, way, piece)
+            held[...] = value.astype(jnp.bfloat16)
+            copy(t, way, piece, held).start()
+        return carry
+
+    lax.fori_loop(1, n - 1, step, 0)
+    for way, piece in LANES:
+        sum_ref[piece * size : (piece + 1) * size, way * half : (way + 1) * half] = total(
+            n - 1, way, piece
+        ).astype(jnp.bfloat16)
+
+    def finish(t, carry):
+        for way, piece in LANES:
+            copy(t, way, piece, slot(t, way, piece)).wait_send()
+        return carry
+
+    lax.fori_loop(0, n - 1, finish, 0)
+
+
+def gather(tail, n):
+    half = tail.shape[1] // 2
+    sems = pltpu.SemaphoreType.DMA((2, PIECES, n - 1))
+    return pl.pallas_call(
+        functools.partial(gather_ring, n, half),
+        out_shape=jax.ShapeDtypeStruct((n * TOK, 2 * half), tail.dtype),
+        in_specs=[pl.BlockSpec(memory_space=pl.ANY)],
+        out_specs=pl.BlockSpec(memory_space=pl.ANY),
+        scratch_shapes=[sems, sems, pltpu.SemaphoreType.DMA],
+        compiler_params=pltpu.CompilerParams(collective_id=0, has_side_effects=True),
+        name="gather_ring",
+    )(tail)
+
+
+def reduce_scatter(terms, n):
+    half = terms.shape[1] // 2
+    sems = pltpu.SemaphoreType.DMA((2, PIECES, n - 1))
+    return pl.pallas_call(
+        functools.partial(reduce_ring, n, half),
+        out_shape=jax.ShapeDtypeStruct((TOK, 2 * half), terms.dtype),
+        in_specs=[pl.BlockSpec(memory_space=pltpu.VMEM)],
+        out_specs=pl.BlockSpec(memory_space=pltpu.VMEM),
+        scratch_shapes=[pltpu.VMEM((n - 1, 2, TOK, half), terms.dtype), sems, sems],
+        compiler_params=pltpu.CompilerParams(
+            collective_id=1, has_side_effects=True, vmem_limit_bytes=48 * 1024 * 1024
+        ),
+        name="reduce_ring",
+    )(terms)
+
+
 def shards(query, key, value, output_gradient, kv_index, count):
     nseq, nhead = lax.axis_size("seq"), lax.axis_size("head")
     shard, part = lax.axis_index("seq"), lax.axis_index("head")
@@ -254,7 +417,7 @@
         near = lax.ppermute(last, "head", up)
         tail = lax.all_gather(last, "head", axis=0)[nhead - 1]
     gathered = [
-        lax.all_gather(tail[:, c * cols : (c + 1) * cols], "seq", axis=0, tiled=True)
+        gather(tail[:, c * cols : (c + 1) * cols], nseq)
         for c in range(CHUNKS)
     ]
     earlier = ()
@@ -265,9 +428,7 @@
             near[:, c * cols : (c + 1) * cols], gathered[c], earlier,
         )
         near_grads.append(near_grad)
-        tail_grads.append(
-            lax.psum_scatter(tail_grad, "seq", scatter_dimension=0, tiled=True)
-        )
+        tail_grads.append(reduce_scatter(tail_grad, nseq))
     attn, dquery, dkey, dvalue = earlier
     near_grad = jnp.concatenate(near_grads, axis=1)
     tail_grad = jnp.concatenate(tail_grads, axis=1)

time: 305 us -> 215 us (0.70)
  waiting for transfers between devices: 205 us -> 24.6 us
  Pallas kernels: 63.2 us -> 168 us
  between operations: 14.2 us -> 0.75 us
    pallas_call x0 -> x2, Pallas kernels: none -> 105 us  [the longest x1 53.1 us: reduce_scatter(): pl.pallas_call(functools.partial(reduce_ring, n, half), out_shape=jax.Sha...]
    reduce_scatter x1 -> x0, waiting for transfers between devices: 103 us -> none  [shards(): lax.psum_scatter(tail_grad, 'seq', scatter_dimension=0, tiled=True)]
    all_gather x1 -> x0, waiting for transfers between devices: 75.8 us -> none  [shards(): lax.all_gather(tail[:, c * cols:(c + 1) * cols], 'seq', axis=0, tiled=True)]
  transfers between devices with their start and end apart: 4 -> 2, of which waited for: 4 -> 2; matrix products, arithmetic and copies ran while one was open for 0% -> 0% of each run, Pallas kernels for 0% -> 0%
where the time goes in v2:
time: 215 us
  Pallas kernels  168 us (78%)
  waiting for transfers between devices  24.6 us (11%)
  local copies, waits for them, and re-layouts  11.9 us (6%)
  other arithmetic  5.28 us (2%)
  starting transfers between devices  4.31 us (2%)
    pallas_call x1, Pallas kernels, call(): pl.pallas_call(functools.partial(attend, nb, nseq, query_group), out_shap...  63.2 us
    pallas_call x1, Pallas kernels, reduce_scatter(): pl.pallas_call(functools.partial(reduce_ring, n, half), out_shape=jax.Sha...  53.1 us
    pallas_call x1, Pallas kernels, gather(): pl.pallas_call(functools.partial(gather_ring, n, half), out_shape=jax.Sha...  52.1 us
    ppermute x1, waiting for transfers between devices, shards(): lax.ppermute(jnp.where(part == 0, tail_grad, near_grad), 'head', pair)  13.2 us
    ppermute x1, waiting for transfers between devices, shards(): near = lax.ppermute(last, 'head', pair)  11.3 us
    slice x1, local copies, waits for them, and re-layouts, shards(): dvalue = dvalue.at[rows - TOK:].add(add[:, :, 1].reshape(TOK, width_kv))  4.53 us
  transfers between devices with their start and end apart: 2, of which 2 were waited for; matrix products, arithmetic and copies ran while one was open for 0% of the time, Pallas kernels for 0%

profile of v2, /device:TPU:0, one launch (start us, length us, event | category | flops | bytes accessed | tf_op | source)
XLA Modules:
  0.0 215.2 jit_solution(6524982323777955759)
XLA Ops:
  0.6 0.0 copy-start
  0.6 1.0 slice.61
  1.6 0.2 stack_reshape.8
  1.9 0.0 copy-start.5
  1.9 1.0 slice.62
  2.9 0.2 stack_reshape.9
  3.1 1.2 pad_maximum_fusion
  4.3 0.4 reshape.75
  4.7 3.0 %collective-permute-start = (bf16[128,2048]{1,0:T(8,128)(2,1)S(1)}, bf16[128,2048]{1,0:T(8,128)(2,1)S(1)}, u32[]{:S(2)}, u32[]{:S(2)}) collective-permute-start(bf16[128,2048]{1,0:T(8,128)(2,1)S(1)} %reshape.75), channel_id=1, source_target_pairs={{0,16},{16,0},{1,17},{17,1},{2,18},{18,2},{3,19},{19,3},{4,20},{20... | collective-permute-start | bytes 1572872 | tf_op jit(solution)/shard_map/ppermute | solution.py:414
  7.7 0.0 copy-done
  7.7 0.1 constant_dynamic-slice_fusion
  7.8 0.0 copy-done.5
  7.8 0.1 convert_bitcast_fusion.3
  7.9 0.1 convert_bitcast_fusion.2
  8.0 0.1 select_bitcast_fusion
  8.1 0.1 copy.10
  8.2 0.1 reshape.74
  8.3 0.1 pad_add_fusion.1.meta
  8.3 11.3 %collective-permute-done.near_ref = bf16[128,2048]{1,0:T(8,128)(2,1)S(1)} collective-permute-done((bf16[128,2048]{1,0:T(8,128)(2,1)S(1)}, bf16[128,2048]{1,0:T(8,128)(2,1)S(1)}, u32[]{:S(2)}, u32[]{:S(2)}) %collective-permute-start) | collective-permute-done | bytes 524320 | tf_op jit(solution)/shard_map/ppermute | solution.py:414
  19.7 0.8 broadcast_select_fusion.1.tail_ref
  20.5 52.1 %gather_ring.1.tail_ref = bf16[2048,2048]{1,0:T(8,128)(2,1)} custom-call(bf16[128,2048]{1,0:T(8,128)(2,1)} %broadcast_select_fusion.1.tail_ref), custom_call_target="tpu_custom_call" | custom-call | tf_op jit(solution)/shard_map/gather_ring/pallas_call | solution.py:356
  72.6 0.0 copy-start.2
  72.6 1.2 copy-done.2
  73.9 0.0 copy-start.3
  73.9 1.2 copy-done.3
  75.1 63.2 %attend.1 = (bf16[512,8192]{1,0:T(8,128)(2,1)}, bf16[512,8192]{1,0:T(8,128)(2,1)}, f32[512,1024]{1,0:T(8,128)S(1)}, f32[512,1024]{1,0:T(8,128)}, bf16[128,2048]{...) custom-call(s32[14]{0:T(128)S(1)} %pad_add_fusion.1.meta, bf16[512,8192]{1,0:T(8,128)(2,1)} %bitcast.42, ...), custom_call_target="tpu_custom_call" | custom-call | flops 19327352832 | bytes 33554432 | tf_op jit(solution)/shard_map/attend/pallas_call | solution.py:186
  138.3 53.1 %reduce_ring.1 = bf16[128,2048]{1,0:T(8,128)(2,1)S(1)} custom-call(bf16[2048,2048]{1,0:T(8,128)(2,1)} %get-tuple-element.37.term_ref), custom_call_target="tpu_custom_call" | custom-call | tf_op jit(solution)/shard_map/reduce_ring/pallas_call | solution.py:370
  191.4 0.1 broadcast_select_fusion
  191.4 1.3 collective-permute-start.1
  192.7 13.2 %collective-permute-done.1 = bf16[128,2048]{1,0:T(8,128)(2,1)S(1)} collective-permute-done((bf16[128,2048]{1,0:T(8,128)(2,1)S(1)}, bf16[128,2048]{1,0:T(8,128)(2,1)S(1)}, u32[]{:S(2)}, u32[]{:S(2)}) %collective-permute-start.1) | collective-permute-done | bytes 524320 | tf_op jit(solution)/shard_map/ppermute | solution.py:436
  206.0 0.2 select_add_fusion
  206.1 1.9 reshape.76
  208.0 0.0 copy-start.4
  208.0 4.5 %slice_reduce_fusion = (f32[128,8,128]{2,1,0:T(8,128)S(1)}, f32[128,8,128]{2,1,0:T(8,128)S(1)}) fusion(f32[128,8,2,128]{3,2,1,0:T(2,128)} %reshape.76), kind=kLoop, calls=%fused_computation.7 | loop fusion | bytes 2097152 | tf_op jit(solution)/shard_map/slice | solution.py:444
  212.5 0.0 copy-done.4
  212.5 0.4 fusion
  212.9 0.0 copy-start.1
  213.0 1.1 convert_bitcast_fusion
  214.1 1.1 convert_bitcast_fusion.1
  215.2 0.0 copy-done.1
  (1 shorter events, 0.0 us)
Async XLA Ops:
  0.6 7.1 %copy-start = (s32[128,3]{0,1:T(4,128)S(1)}, s32[128,3]{0,1:T(4,128)}, u32[]{:S(2)}) copy-start(s32[128,3]{0,1:T(4,128)} %param.14) | copy-start | bytes 4612
  1.9 5.9 %copy-start.5 = (s32[128]{0:T(128)S(1)}, s32[128]{0:T(128)}, u32[]{:S(2)}) copy-start(s32[128]{0:T(128)} %param.15) | copy-start | bytes 1540
  4.7 15.0 %collective-permute-start = (bf16[128,2048]{1,0:T(8,128)(2,1)S(1)}, bf16[128,2048]{1,0:T(8,128)(2,1)S(1)}, u32[]{:S(2)}, u32[]{:S(2)}) collective-permute-start(bf16[128,2048]{1,0:T(8,128)(2,1)S(1)} %reshape.75), channel_id=1, source_target_pairs={{0,16},{16,0},{1,17},{17,1},{2,18},{18,2},{3,19},{19,3},{4,20},{20... | collective-permute-start | bytes 1572872 | tf_op jit(solution)/shard_map/ppermute | solution.py:414
  72.6 1.2 copy-start.2
  73.9 1.2 copy-start.3
  191.4 14.5 %collective-permute-start.1 = (bf16[128,2048]{1,0:T(8,128)(2,1)S(1)}, bf16[128,2048]{1,0:T(8,128)(2,1)S(1)}, u32[]{:S(2)}, u32[]{:S(2)}) collective-permute-start(bf16[128,2048]{1,0:T(8,128)(2,1)S(1)} %broadcast_select_fusion), channel_id=1, source_target_pairs={{0,16},{16,0},{1,17},{17,1},{2,18},{18,2},{3,19},{19,3},{4,20},{20... | collective-permute-start | bytes 1572872 | tf_op jit(solution)/shard_map/ppermute | solution.py:436
  208.0 4.5 %copy-start.4 = (f32[512,1024]{1,0:T(8,128)S(1)}, f32[512,1024]{1,0:T(8,128)}, u32[]{:S(2)}) copy-start(f32[512,1024]{1,0:T(8,128)} %get-tuple-element.39) | copy-start | bytes 6291460
  212.9 2.3 %copy-start.1 = (s32[128,3]{0,1:T(4,128)S(1)}, s32[128,3]{0,1:T(4,128)}, u32[]{:S(2)}) copy-start(s32[128,3]{0,1:T(4,128)} %param.14) | copy-start | bytes 4612

commit v3 on v2

--- a/solution.py
+++ b/solution.py
@@ -217,7 +217,7 @@
     )(meta, *operands)
 
 
-PIECES = 2
+PIECES = 4
 
 
 def ring_place(n):

time: 215 us -> 212 us (0.986)
  Pallas kernels: 168 us -> 164 us
    pallas_call x1, Pallas kernels: 52.1 us -> 49.3 us  [gather(): pl.pallas_call(functools.partial(gather_ring, n, half), out_shape=jax.Sha...]
where the time goes in v3:
time: 212 us
  Pallas kernels  164 us (77%)
  waiting for transfers between devices  24.6 us (12%)
  local copies, waits for them, and re-layouts  11.9 us (6%)
  other arithmetic  5.28 us (2%)
  starting transfers between devices  4.62 us (2%)
    pallas_call x1, Pallas kernels, call(): pl.pallas_call(functools.partial(attend, nb, nseq, query_group), out_shap...  63.2 us
    pallas_call x1, Pallas kernels, reduce_scatter(): pl.pallas_call(functools.partial(reduce_ring, n, half), out_shape=jax.Sha...  51.8 us
    pallas_call x1, Pallas kernels, gather(): pl.pallas_call(functools.partial(gather_ring, n, half), out_shape=jax.Sha...  49.3 us
    ppermute x1, waiting for transfers between devices, shards(): lax.ppermute(jnp.where(part == 0, tail_grad, near_grad), 'head', pair)  13.2 us
    ppermute x1, waiting for transfers between devices, shards(): near = lax.ppermute(last, 'head', pair)  11.3 us
    slice x1, local copies, waits for them, and re-layouts, shards(): dvalue = dvalue.at[rows - TOK:].add(add[:, :, 1].reshape(TOK, width_kv))  4.53 us
  transfers between devices with their start and end apart: 2, of which 2 were waited for; matrix products, arithmetic and copies ran while one was open for 0% of the time, Pallas kernels for 0%

profile of v3, /device:TPU:0, one launch (start us, length us, event | category | flops | bytes accessed | tf_op | source)
XLA Modules:
  0.0 211.5 jit_solution(12606839917587218427)
XLA Ops:
  0.6 0.0 copy-start
  0.6 1.0 slice.61
  1.6 0.2 stack_reshape.8
  1.9 0.0 copy-start.5
  1.9 1.0 slice.62
  2.9 0.2 stack_reshape.9
  3.1 1.2 pad_maximum_fusion
  4.3 0.4 reshape.75
  4.7 3.0 %collective-permute-start = (bf16[128,2048]{1,0:T(8,128)(2,1)S(1)}, bf16[128,2048]{1,0:T(8,128)(2,1)S(1)}, u32[]{:S(2)}, u32[]{:S(2)}) collective-permute-start(bf16[128,2048]{1,0:T(8,128)(2,1)S(1)} %reshape.75), channel_id=1, source_target_pairs={{0,16},{16,0},{1,17},{17,1},{2,18},{18,2},{3,19},{19,3},{4,20},{20... | collective-permute-start | bytes 1572872 | tf_op jit(solution)/shard_map/ppermute | solution.py:414
  7.7 0.0 copy-done
  7.7 0.1 constant_dynamic-slice_fusion
  7.8 0.0 copy-done.5
  7.8 0.1 convert_bitcast_fusion.3
  7.9 0.1 convert_bitcast_fusion.2
  8.0 0.1 select_bitcast_fusion
  8.1 0.1 copy.10
  8.2 0.1 reshape.74
  8.3 0.1 pad_add_fusion.1.meta
  8.3 11.3 %collective-permute-done.near_ref = bf16[128,2048]{1,0:T(8,128)(2,1)S(1)} collective-permute-done((bf16[128,2048]{1,0:T(8,128)(2,1)S(1)}, bf16[128,2048]{1,0:T(8,128)(2,1)S(1)}, u32[]{:S(2)}, u32[]{:S(2)}) %collective-permute-start) | collective-permute-done | bytes 524320 | tf_op jit(solution)/shard_map/ppermute | solution.py:414
  19.7 0.8 broadcast_select_fusion.1.tail_ref
  20.5 49.3 %gather_ring.1.tail_ref = bf16[2048,2048]{1,0:T(8,128)(2,1)} custom-call(bf16[128,2048]{1,0:T(8,128)(2,1)} %broadcast_select_fusion.1.tail_ref), custom_call_target="tpu_custom_call" | custom-call | tf_op jit(solution)/shard_map/gather_ring/pallas_call | solution.py:356
  69.9 0.0 copy-start.2
  69.9 1.2 copy-done.2
  71.1 0.0 copy-start.3
  71.1 1.2 copy-done.3
  72.3 63.2 %attend.1 = (bf16[512,8192]{1,0:T(8,128)(2,1)}, bf16[512,8192]{1,0:T(8,128)(2,1)}, f32[512,1024]{1,0:T(8,128)S(1)}, f32[512,1024]{1,0:T(8,128)}, bf16[128,2048]{...) custom-call(s32[14]{0:T(128)S(1)} %pad_add_fusion.1.meta, bf16[512,8192]{1,0:T(8,128)(2,1)} %bitcast.42, ...), custom_call_target="tpu_custom_call" | custom-call | flops 19327352832 | bytes 33554432 | tf_op jit(solution)/shard_map/attend/pallas_call | solution.py:186
  135.5 51.8 %reduce_ring.1 = bf16[128,2048]{1,0:T(8,128)(2,1)S(1)} custom-call(bf16[2048,2048]{1,0:T(8,128)(2,1)} %get-tuple-element.37.term_ref), custom_call_target="tpu_custom_call" | custom-call | tf_op jit(solution)/shard_map/reduce_ring/pallas_call | solution.py:370
  187.4 0.1 broadcast_select_fusion
  187.4 1.6 collective-permute-start.1
  189.0 13.2 %collective-permute-done.1 = bf16[128,2048]{1,0:T(8,128)(2,1)S(1)} collective-permute-done((bf16[128,2048]{1,0:T(8,128)(2,1)S(1)}, bf16[128,2048]{1,0:T(8,128)(2,1)S(1)}, u32[]{:S(2)}, u32[]{:S(2)}) %collective-permute-start.1) | collective-permute-done | bytes 524320 | tf_op jit(solution)/shard_map/ppermute | solution.py:436
  202.3 0.2 select_add_fusion
  202.4 1.9 reshape.76
  204.3 0.0 copy-start.4
  204.3 4.5 %slice_reduce_fusion = (f32[128,8,128]{2,1,0:T(8,128)S(1)}, f32[128,8,128]{2,1,0:T(8,128)S(1)}) fusion(f32[128,8,2,128]{3,2,1,0:T(2,128)} %reshape.76), kind=kLoop, calls=%fused_computation.7 | loop fusion | bytes 2097152 | tf_op jit(solution)/shard_map/slice | solution.py:444
  208.8 0.0 copy-done.4
  208.8 0.4 fusion
  209.2 0.0 copy-start.1
  209.2 1.1 convert_bitcast_fusion
  210.4 1.1 convert_bitcast_fusion.1
  211.5 0.0 copy-done.1
  (1 shorter events, 0.0 us)
Async XLA Ops:
  0.6 7.1 %copy-start = (s32[128,3]{0,1:T(4,128)S(1)}, s32[128,3]{0,1:T(4,128)}, u32[]{:S(2)}) copy-start(s32[128,3]{0,1:T(4,128)} %param.14) | copy-start | bytes 4612
  1.9 5.9 %copy-start.5 = (s32[128]{0:T(128)S(1)}, s32[128]{0:T(128)}, u32[]{:S(2)}) copy-start(s32[128]{0:T(128)} %param.15) | copy-start | bytes 1540
  4.7 15.0 %collective-permute-start = (bf16[128,2048]{1,0:T(8,128)(2,1)S(1)}, bf16[128,2048]{1,0:T(8,128)(2,1)S(1)}, u32[]{:S(2)}, u32[]{:S(2)}) collective-permute-start(bf16[128,2048]{1,0:T(8,128)(2,1)S(1)} %reshape.75), channel_id=1, source_target_pairs={{0,16},{16,0},{1,17},{17,1},{2,18},{18,2},{3,19},{19,3},{4,20},{20... | collective-permute-start | bytes 1572872 | tf_op jit(solution)/shard_map/ppermute | solution.py:414
  69.9 1.2 copy-start.2
  71.1 1.2 copy-start.3
  187.4 14.8 %collective-permute-start.1 = (bf16[128,2048]{1,0:T(8,128)(2,1)S(1)}, bf16[128,2048]{1,0:T(8,128)(2,1)S(1)}, u32[]{:S(2)}, u32[]{:S(2)}) collective-permute-start(bf16[128,2048]{1,0:T(8,128)(2,1)S(1)} %broadcast_select_fusion), channel_id=1, source_target_pairs={{0,16},{16,0},{1,17},{17,1},{2,18},{18,2},{3,19},{19,3},{4,20},{20... | collective-permute-start | bytes 1572872 | tf_op jit(solution)/shard_map/ppermute | solution.py:436
  204.3 4.5 %copy-start.4 = (f32[512,1024]{1,0:T(8,128)S(1)}, f32[512,1024]{1,0:T(8,128)}, u32[]{:S(2)}) copy-start(f32[512,1024]{1,0:T(8,128)} %get-tuple-element.39) | copy-start | bytes 6291460
  209.2 2.3 %copy-start.1 = (s32[128,3]{0,1:T(4,128)S(1)}, s32[128,3]{0,1:T(4,128)}, u32[]{:S(2)}) copy-start(s32[128,3]{0,1:T(4,128)} %param.14) | copy-start | bytes 4612
